TPU v7x, 32 devices: a whole 2x2x4 slice. The times are simulated.
32 devices in a mesh: inner: 16 (over z, y, x), outer: 2 (over core).
Axes of the slice: x: 2, y: 2, z: 4, core: 2. Of those that a mesh axis runs over, the one named last changes fastest.
Arguments:
- feats_first: bfloat16 [2, 4096, 2048], P('outer', 'inner'), may hold values from -4 to 8
- feats_second: bfloat16 [2, 4096, 2048], P('outer', 'inner'), may hold values from -4 to 8
- expander: bfloat16 [2048, 1024], P('inner'), may hold values from -0.125 to 0.125
- tile_count: int32 [2, 16], replicated, may hold values from 64 to 256, as said below
- match_dev: int32 [2, 4096, 1], P('outer', 'inner'), may hold values from 0 to 15; in each aligned block of 256 rows (0 to 255, 256 to 511, ..., all dimensions but the last counted through in order) at most 48 rows name the same one
- match_tile: int32 [2, 4096], P('outer', 'inner'), may hold values from 0 to 255
Outputs:
- covariance: float32 [1024, 1024], P('inner')
- invariance: float32 [2, 4096], P('outer', 'inner')
Inputs may be any that keep to these rules, and one draw needn't show every extreme that they name: `tile_count`: for every slide some device has all 256 tiles live; the others at least a quarter. `match_dev`: at most 48 tiles of one device name the same device.
All inputs are finite; a program needn't handle non-finite values.
Results may differ from a plain program's by a relative error of at most 0.00135.
Values may be sent and summed in bfloat16 or wider, within the bound.
A program may use at most 64 MiB of HBM per device.

v0:
```python
import jax
import jax.numpy as jnp
from jax import lax
from jax.sharding import PartitionSpec as P


def shards(feats_first, feats_second, expander, tile_count, match_dev, match_tile):
    first_rows = feats_first[0]
    second_rows = feats_second[0]
    tile_rows = first_rows.shape[0]
    expand_width = expander.shape[1]
    group_size = lax.axis_size("inner")
    capacity = max(2, 3 * tile_rows // group_size)
    inner_pos = lax.axis_index("inner")
    outer_pos = lax.axis_index("outer")
    piece = lax.all_gather(expander, "inner", axis=0, tiled=True)
    first_acc = jnp.dot(first_rows, piece, preferred_element_type=jnp.float32)
    second_acc = jnp.dot(second_rows, piece, preferred_element_type=jnp.float32)
    first_embed = first_acc.astype(jnp.bfloat16)
    second_embed = second_acc.astype(jnp.bfloat16)
    counts = lax.dynamic_index_in_dim(tile_count, outer_pos, 0, keepdims=False)
    own_count = lax.dynamic_index_in_dim(counts, inner_pos, 0, keepdims=False)
    row_index = jnp.arange(tile_rows, dtype=jnp.int32)
    live = row_index < own_count
    target_dev = match_dev[0, :, 0]
    target_tile = match_tile[0]
    onehot = (target_dev[:, None] == jnp.arange(group_size, dtype=jnp.int32)[None, :]).astype(
        jnp.int32
    )
    slot_pos = jnp.sum((jnp.cumsum(onehot, axis=0) - 1) * onehot, axis=1)
    send_rows = (
        jnp.zeros((group_size, capacity, expand_width), jnp.bfloat16)
        .at[target_dev, slot_pos]
        .set(first_embed)
    )
    send_tiles = (
        jnp.zeros((group_size, capacity), jnp.int32).at[target_dev, slot_pos].set(target_tile)
    )
    recv_rows, recv_tiles = (
        lax.all_to_all(send_rows, "inner", split_axis=0, concat_axis=0, tiled=True),
        lax.all_to_all(send_tiles, "inner", split_axis=0, concat_axis=0, tiled=True),
    )
    partner = second_embed[recv_tiles]
    diff = recv_rows.astype(jnp.float32) - partner.astype(jnp.float32)
    distance = jnp.where(recv_tiles < own_count, jnp.mean(diff * diff, axis=-1), jnp.float32(0.0))
    returned = lax.all_to_all(distance, "inner", split_axis=0, concat_axis=0, tiled=True)
    dest_count = counts[target_dev]
    valid = live & (target_tile < dest_count)
    invariance = jnp.where(valid, returned[target_dev, slot_pos], jnp.float32(0.0))
    masked = jnp.where(live[:, None], first_embed, jnp.zeros_like(first_embed))
    column_total = lax.psum(jnp.sum(masked.astype(jnp.float32), axis=0), ("inner", "outer"))
    total = jnp.sum(tile_count).astype(jnp.float32)
    share_rows = expand_width // group_size
    local_share = lax.psum_scatter(
        lax.dot_general(
            masked, masked, (((0,), (0,)), ((), ())), preferred_element_type=jnp.float32
        ),
        "inner",
        scatter_dimension=0,
        tiled=True,
    )
    gram_share = lax.psum(local_share, "outer")
    own_sums = lax.dynamic_slice_in_dim(column_total, inner_pos * share_rows, share_rows, 0)
    covariance = (gram_share - own_sums[:, None] * column_total[None, :] / total) / (total - 1.0)
    return (covariance, invariance[None, :])


def solution(mesh):
    return jax.shard_map(
        shards,
        mesh=mesh,
        in_specs=(
            P("outer", "inner", None),
            P("outer", "inner", None),
            P("inner", None),
            P(),
            P("outer", "inner", None),
            P("outer", "inner"),
        ),
        out_specs=(P("inner", None), P("outer", "inner")),
        check_vma=False,
    )
```

profile of v0, /device:TPU:0, one launch (start us, length us, event | category | flops | bytes accessed | tf_op | source)
XLA Modules:
  0.0 292.9 jit_solution(2286077928159644080)
XLA Ops:
  7.2 0.7 all-gather.2.cloned.1.call-update
  8.0 1.3 dynamic_slice.11
  9.3 0.6 iota_compare_fusion.2
  10.0 79.6 %all-gather.2.cloned.1.call-done = bf16[2048,1024]{1,0:T(8,128)(2,1)} async-done(((bf16[128,1024]{1,0:T(8,128)(2,1)}), bf16[2048,1024]{1,0:T(8,128)(2,1)}) %all-gather.2.cloned.1.call-update) | async-done | bytes 4194320 | tf_op jit(solution)/shard_map/all_gather | solution.py:16
  89.6 3.4 %convert_reduce_fusion = (f32[1024]{0:T(1024)S(1)}, bf16[256,1024]{1,0:T(8,128)(2,1)S(1)}) fusion(pred[256]{0:T(512)(128)(4,1)S(1)} %iota_compare_fusion.2, bf16[2048,1024]{1,0:T(8,128)(2,1)} %all-gather.2.cloned.1.call-done, bf16[1,256,2048]{2,1,0:T(8,128)(2,1)S(1)} %copy-done), kind=kOutput, calls=%fused_computation.11 | convolution fusion | flops 1074789376 | bytes 5771520 | tf_op jit(solution)/shard_map/dot_general | solution.py:17
  93.1 2.8 fusion.4
  95.9 0.6 copy-done.1
  96.5 0.6 reduce-window.6
  97.1 0.2 slice_reduce_fusion
  97.3 0.7 fusion.11
  98.1 0.1 fusion.6
  98.1 4.3 %compare_select_fusion.4 = (s32[256,1]{0,1:T(1,128)S(1)}, s32[256,1]{0,1:T(1,128)S(1)}) fusion(s32[]{:T(128)} %bitcast.12, s32[]{:T(128)} %bitcast.13, s32[]{:T(128)} %bitcast.14, s32[]{:T(128)} %bitcast.15, s32[]{:T(128)} %bitcast.16, s32[]{:T(128)} %bitcast.18, s32[]{:T(128)} %bitcast.17, s32[1,256,1]{1,2,0:T(1,128)S(1)} %copy-done.1), kind=kLoop, calls=%fused_computation.38 | loop fusion | flops 3840 | bytes 3100 | tf_op jit(solution)/shard_map/gather | solution.py:47
  102.4 0.6 broadcast.105
  103.0 36.1 %scatter_fusion = s32[16,48]{1,0:T(8,128)} fusion(s32[16,48]{1,0:T(8,128)} %broadcast.105, s32[256]{0:T(256)S(1)} %bitcast.67, s32[256]{0:T(256)S(1)} %bitcast.75), kind=kCustom, calls=%fused_computation.2 | custom fusion | bytes 5120 | tf_op jit(solution)/shard_map/scatter | solution.py:37
  139.2 4.4 %all-to-all-start = ((s32[16,1,48]{2,1,0:T(1,128)}), s32[16,1,48]{2,1,0:T(1,128)S(1)}, u32[]{:S(2)}, u32[]{:S(2)}) async-start(s32[16,1,48]{2,1,0:T(1,128)} %bitcast.28), calls=%async_computation.1 | async-start | bytes 16384 | tf_op jit(solution)/shard_map/all_to_all | solution.py:41
  143.6 1.4 broadcast_in_dim.22
  145.0 36.8 %scatter_fusion.1 = bf16[16,48,1024]{2,1,0:T(8,128)(2,1)} fusion(bf16[16,48,1024]{2,1,0:T(8,128)(2,1)} %broadcast_in_dim.22, s32[256]{0:T(256)S(1)} %bitcast.68, bf16[256,1024]{1,0:T(8,128)(2,1)S(1)} %get-tuple-element.32), kind=kCustom, calls=%fused_computation.3 | custom fusion | bytes 1574912 | tf_op jit(solution)/shard_map/scatter | solution.py:34
  181.8 7.1 %all-to-all-start.1 = ((bf16[16,48,1024]{2,1,0:T(8,128)(2,1)}), bf16[16,48,1024]{2,1,0:T(8,128)(2,1)S(1)}, u32[]{:S(2)}, u32[]{:S(2)}) async-start(bf16[16,48,1024]{2,1,0:T(8,128)(2,1)} %scatter_fusion.1), calls=%async_computation.2 | async-start | bytes 3145728 | tf_op jit(solution)/shard_map/all_to_all | solution.py:40
  189.0 0.1 reshape.148
  189.0 3.8 %convolution_convert_fusion = bf16[256,1024]{1,0:T(8,128)(2,1)S(1)} fusion(bf16[2048,1024]{1,0:T(8,128)(2,1)} %all-gather.2.cloned.1.call-done, bf16[1,256,2048]{2,1,0:T(8,128)(2,1)} %param.7), kind=kOutput, calls=%fused_computation.7 | convolution fusion | flops 1074003968 | bytes 5767168 | tf_op jit(solution)/shard_map/dot_general | solution.py:18
  192.8 3.6 %gather_fusion = bf16[768,1024]{1,0:T(8,128)(2,1)} fusion(bf16[256,1024]{1,0:T(8,128)(2,1)S(1)} %convolution_convert_fusion, s32[1024]{0:T(1024)S(1)} %pad_clamp_fusion), kind=kCustom, calls=%fused_computation | custom fusion | bytes 3148800 | tf_op jit(solution)/shard_map/gather | solution.py:43
  196.4 26.0 %all-to-all-done.1 = bf16[16,48,1024]{2,1,0:T(8,128)(2,1)S(1)} async-done(((bf16[16,48,1024]{2,1,0:T(8,128)(2,1)}), bf16[16,48,1024]{2,1,0:T(8,128)(2,1)S(1)}, u32[]{:S(2)}, u32[]{:S(2)}) %all-to-all-start.1) | async-done | bytes 1572896 | tf_op jit(solution)/shard_map/all_to_all | solution.py:40
  222.4 2.0 fusion.1
  224.4 1.2 compare_select_fusion
  225.6 7.3 %all-to-all-start.2 = ((f32[16,1,48]{2,1,0:T(1,128)}), f32[16,1,48]{2,1,0:T(1,128)S(1)}, u32[]{:S(2)}, u32[]{:S(2)}) async-start(f32[16,1,48]{2,1,0:T(1,128)} %compare_select_fusion), calls=%async_computation.3 | async-start | bytes 16384 | tf_op jit(solution)/shard_map/all_to_all | solution.py:46
  233.0 0.7 all-reduce.2.cloned.1.call-update
  233.7 5.6 %select_select_fusion = s32[256]{0:T(256)S(1)} fusion(pred[256]{0:T(512)(128)(4,1)S(1)} %get-tuple-element.10, pred[256]{0:T(512)(128)(4,1)S(1)} %get-tuple-element.9, pred[256]{0:T(512)(128)(4,1)S(1)} %get-tuple-element.8, pred[256]{0:T(512)(128)(4,1)S(1)} %get-tuple-element.7, pred[256]{0:T(512)(128)(4,1)S(1)} %get-tuple-element.6, ...), kind=kLoop, calls=%fused_computation.49 | loop fusion | flops 2304 | bytes 4388 | tf_op jit(solution)/shard_map/gather | solution.py:47
  239.3 0.6 reduce_sum.39
  240.6 40.7 %psum.15 = f32[1024]{0:T(1024)S(1)} all-reduce(f32[1024]{0:T(1024)S(1)} %get-tuple-element.31), channel_id=1, replica_groups=mesh['inner'=16,'outer'=2] {'inner','outer'}, use_global_device_ids=true, to_apply=%region_3.4 | all-reduce | flops 1024 | bytes 8192 | tf_op jit(solution)/shard_map/psum | solution.py:51
  281.4 1.9 gather_fusion.1
  283.4 1.2 and_select_fusion
  284.6 1.8 subtract_divide_fusion
  (25 shorter events, 0.4 us)
Async XLA Ops:
  7.2 82.4 %copy-start = (bf16[1,256,2048]{2,1,0:T(8,128)(2,1)S(1)}, bf16[1,256,2048]{2,1,0:T(8,128)(2,1)}, u32[]{:S(2)}) copy-start(bf16[1,256,2048]{2,1,0:T(8,128)(2,1)} %param.6) | copy-start | bytes 3145732
  7.2 82.4 %all-gather.2.cloned.1.call-start = ((), (), s32[]{:S(2)}) async-start(), calls=%async_computation.4 | async-start | bytes 4456448 | tf_op jit(solution)/shard_map/all_gather | solution.py:16
  7.9 225.1 %reduce-scatter.2.cloned.1.call-start = ((), (), s32[]{:S(2)}) async-start(), calls=%async_computation.5 | async-start | bytes 4456448 | tf_op jit(solution)/shard_map/reduce_scatter | solution.py:54
  95.8 0.7 copy-start.1
  95.8 1.5 copy-start.3
  95.8 7.2 %copy-start.2 = (s32[1,256]{1,0:T(1,128)S(1)}, s32[1,256]{1,0:T(1,128)}, u32[]{:S(2)}) copy-start(s32[1,256]{1,0:T(1,128)} %param.11) | copy-start | bytes 3076
  139.2 42.6 %all-to-all-start = ((s32[16,1,48]{2,1,0:T(1,128)}), s32[16,1,48]{2,1,0:T(1,128)S(1)}, u32[]{:S(2)}, u32[]{:S(2)}) async-start(s32[16,1,48]{2,1,0:T(1,128)} %bitcast.28), calls=%async_computation.1 | async-start | bytes 16384 | tf_op jit(solution)/shard_map/all_to_all | solution.py:41
  181.8 40.6 %all-to-all-start.1 = ((bf16[16,48,1024]{2,1,0:T(8,128)(2,1)}), bf16[16,48,1024]{2,1,0:T(8,128)(2,1)S(1)}, u32[]{:S(2)}, u32[]{:S(2)}) async-start(bf16[16,48,1024]{2,1,0:T(8,128)(2,1)} %scatter_fusion.1), calls=%async_computation.2 | async-start | bytes 3145728 | tf_op jit(solution)/shard_map/all_to_all | solution.py:40
  225.6 55.8 %all-to-all-start.2 = ((f32[16,1,48]{2,1,0:T(1,128)}), f32[16,1,48]{2,1,0:T(1,128)S(1)}, u32[]{:S(2)}, u32[]{:S(2)}) async-start(f32[16,1,48]{2,1,0:T(1,128)} %compare_select_fusion), calls=%async_computation.3 | async-start | bytes 16384 | tf_op jit(solution)/shard_map/all_to_all | solution.py:46
  233.0 51.6 %all-reduce.2.cloned.1.call-start = ((), (), s32[]{:S(2)}) async-start(), calls=%async_computation.6 | async-start | bytes 524288 | tf_op jit(solution)/shard_map/psum | solution.py:62
Sparse Core Ops, SparseCore 0:
  10.8 78.7 all-gather.1
  96.0 93.7 reduce-scatter.1
  236.1 19.5 all-reduce.1
where the time goes:
time: 296 us; the launch traced here: 293 us
  waiting for transfers between devices  107 us (36%)
  local copies, waits for them, and re-layouts  83.5 us (28%)
  blocking collectives  40.7 us (14%)
  starting transfers between devices  18.9 us (6%)
  other arithmetic  18.1 us (6%)
  between operations  14.5 us (5%)
  matrix products  10 us (3%)
    all_gather x1, waiting for transfers between devices, shards(): piece = lax.all_gather(expander, 'inner', axis=0, tiled=True)  79.6 us
    psum x1, blocking collectives, shards(): lax.psum(jnp.sum(masked.astype(jnp.float32), axis=0), ('inner', 'outer'))  40.7 us
    scatter x1, local copies, waits for them, and re-layouts, shards(): send_rows = jnp.zeros((group_size, capacity, expand_width), jnp.bfloat16)...  36.8 us
    scatter x1, local copies, waits for them, and re-layouts, shards(): jnp.zeros((group_size, capacity), jnp.int32).at[target_dev, slot_pos]  36.1 us
    all_to_all x1, waiting for transfers between devices, shards(): lax.all_to_all(send_rows, 'inner', split_axis=0, concat_axis=0, tiled=True)  26 us
    gather x3, other arithmetic, shards(): dest_count = counts[target_dev]  9.95 us
    all_to_all x1, starting transfers between devices, shards(): lax.all_to_all(distance, 'inner', split_axis=0, concat_axis=0, tiled=True)  7.3 us
    all_to_all x1, starting transfers between devices, shards(): lax.all_to_all(send_rows, 'inner', split_axis=0, concat_axis=0, tiled=True)  7.08 us
  transfers between devices with their start and end apart: 6, of which 2 were waited for; matrix products, arithmetic and copies ran while one was open for 35% of the time, Pallas kernels for 0%

commit v1 on v0

--- a/solution.py
+++ b/solution.py
@@ -1,7 +1,23 @@
+import functools
 import jax
 import jax.numpy as jnp
 from jax import lax
 from jax.sharding import PartitionSpec as P
+
+
+def define_sides(x0, chip_axis):
+    parts_n = lax.axis_size(chip_axis)
+    arr_out = sorted(((at, (at + 1) % parts_n) for at in range(parts_n)))
+    current_arr = x0
+    rows = [current_arr]
+    for h in range(1, parts_n):
+        current_arr = lax.ppermute(current_arr, chip_axis, arr_out)
+        rows.insert(0, current_arr)
+    taken_in = jnp.roll(jnp.concatenate(rows, 0), (lax.axis_index(chip_axis) + 1) * x0.shape[0], 0)
+    return taken_in
+
+
+list_runs = functools.partial(define_sides, chip_axis="inner")
 
 
 def shards(feats_first, feats_second, expander, tile_count, match_dev, match_tile):
@@ -13,7 +29,7 @@
     capacity = max(2, 3 * tile_rows // group_size)
     inner_pos = lax.axis_index("inner")
     outer_pos = lax.axis_index("outer")
-    piece = lax.all_gather(expander, "inner", axis=0, tiled=True)
+    piece = list_runs(expander)
     first_acc = jnp.dot(first_rows, piece, preferred_element_type=jnp.float32)
     second_acc = jnp.dot(second_rows, piece, preferred_element_type=jnp.float32)
     first_embed = first_acc.astype(jnp.bfloat16)

time: 296 us -> 381 us (1.29)
  waiting for transfers between devices: 107 us -> 174 us
  local copies, waits for them, and re-layouts: 83.5 us -> 101 us
    ppermute x0 -> x15, waiting for transfers between devices: none -> 158 us  [define_sides(): current_arr = lax.ppermute(current_arr, chip_axis, arr_out)]
    all_gather x1 -> x0, waiting for transfers between devices: 79.6 us -> none  [shards(): piece = lax.all_gather(expander, 'inner', axis=0, tiled=True)]
    unnamed x8 -> x63, local copies, waits for them, and re-layouts: 0.67 us -> 16.9 us
    all_to_all x1, waiting for transfers between devices: 26 us -> 14.9 us  [shards(): lax.all_to_all(send_rows, 'inner', split_axis=0, concat_axis=0, tiled=True)]
  transfers between devices with their start and end apart: 6 -> 20, of which waited for: 2 -> 16; matrix products, arithmetic and copies ran while one was open for 35% -> 28% of each run, Pallas kernels for 0% -> 0%
where the time goes in v1:
time: 381 us; the launch traced here: 378 us
  waiting for transfers between devices  174 us (46%)
  local copies, waits for them, and re-layouts  101 us (27%)
  blocking collectives  40.7 us (11%)
  starting transfers between devices  19.8 us (5%)
  other arithmetic  18.6 us (5%)
  between operations  15.2 us (4%)
  matrix products  8.77 us (2%)
    ppermute x15, waiting for transfers between devices, define_sides(): current_arr = lax.ppermute(current_arr, chip_axis, arr_out)  158 us
    psum x1, blocking collectives, shards(): lax.psum(jnp.sum(masked.astype(jnp.float32), axis=0), ('inner', 'outer'))  40.7 us
    scatter x1, local copies, waits for them, and re-layouts, shards(): send_rows = jnp.zeros((group_size, capacity, expand_width), jnp.bfloat16)...  36.8 us
    scatter x1, local copies, waits for them, and re-layouts, shards(): jnp.zeros((group_size, capacity), jnp.int32).at[target_dev, slot_pos]  36.1 us
    unnamed x63, local copies, waits for them, and re-layouts  16.9 us
    all_to_all x1, waiting for transfers between devices, shards(): lax.all_to_all(send_rows, 'inner', split_axis=0, concat_axis=0, tiled=True)  14.9 us
    gather x3, other arithmetic, shards(): dest_count = counts[target_dev]  10.2 us
  transfers between devices with their start and end apart: 20, of which 16 were waited for; matrix products, arithmetic and copies ran while one was open for 28% of the time, Pallas kernels for 0%

profile of v1, /device:TPU:0, one launch (start us, length us, event | category | flops | bytes accessed | tf_op | source)
XLA Modules:
  0.0 378.2 jit_solution(13407570571552110974)
XLA Ops:
  7.2 3.0 collective-permute-start
  10.2 10.5 %collective-permute-done = bf16[128,1024]{1,0:T(8,128)(2,1)S(1)} collective-permute-done((bf16[128,1024]{1,0:T(8,128)(2,1)}, bf16[128,1024]{1,0:T(8,128)(2,1)S(1)}, u32[]{:S(2)}, u32[]{:S(2)}) %collective-permute-start) | collective-permute-done | bytes 262176 | tf_op jit(solution)/shard_map/ppermute | solution.py:14
  20.7 11.1 %collective-permute-done.1 = bf16[128,1024]{1,0:T(8,128)(2,1)S(1)} collective-permute-done((bf16[128,1024]{1,0:T(8,128)(2,1)S(1)}, bf16[128,1024]{1,0:T(8,128)(2,1)S(1)}, u32[]{:S(2)}, u32[]{:S(2)}) %collective-permute-start.1) | collective-permute-done | bytes 262176 | tf_op jit(solution)/shard_map/ppermute | solution.py:14
  31.8 10.2 %collective-permute-done.2 = bf16[128,1024]{1,0:T(8,128)(2,1)S(1)} collective-permute-done((bf16[128,1024]{1,0:T(8,128)(2,1)S(1)}, bf16[128,1024]{1,0:T(8,128)(2,1)S(1)}, u32[]{:S(2)}, u32[]{:S(2)}) %collective-permute-start.2) | collective-permute-done | bytes 262176 | tf_op jit(solution)/shard_map/ppermute | solution.py:14
  42.0 10.0 %collective-permute-done.3 = bf16[128,1024]{1,0:T(8,128)(2,1)S(1)} collective-permute-done((bf16[128,1024]{1,0:T(8,128)(2,1)S(1)}, bf16[128,1024]{1,0:T(8,128)(2,1)S(1)}, u32[]{:S(2)}, u32[]{:S(2)}) %collective-permute-start.3) | collective-permute-done | bytes 262176 | tf_op jit(solution)/shard_map/ppermute | solution.py:14
  52.0 10.0 %collective-permute-done.4 = bf16[128,1024]{1,0:T(8,128)(2,1)S(1)} collective-permute-done((bf16[128,1024]{1,0:T(8,128)(2,1)S(1)}, bf16[128,1024]{1,0:T(8,128)(2,1)S(1)}, u32[]{:S(2)}, u32[]{:S(2)}) %collective-permute-start.4) | collective-permute-done | bytes 262176 | tf_op jit(solution)/shard_map/ppermute | solution.py:14
  61.9 10.0 %collective-permute-done.5 = bf16[128,1024]{1,0:T(8,128)(2,1)S(1)} collective-permute-done((bf16[128,1024]{1,0:T(8,128)(2,1)S(1)}, bf16[128,1024]{1,0:T(8,128)(2,1)S(1)}, u32[]{:S(2)}, u32[]{:S(2)}) %collective-permute-start.5) | collective-permute-done | bytes 262176 | tf_op jit(solution)/shard_map/ppermute | solution.py:14
  71.9 10.9 %collective-permute-done.6 = bf16[128,1024]{1,0:T(8,128)(2,1)S(1)} collective-permute-done((bf16[128,1024]{1,0:T(8,128)(2,1)S(1)}, bf16[128,1024]{1,0:T(8,128)(2,1)S(1)}, u32[]{:S(2)}, u32[]{:S(2)}) %collective-permute-start.6) | collective-permute-done | bytes 262176 | tf_op jit(solution)/shard_map/ppermute | solution.py:14
  82.8 12.0 %collective-permute-done.7 = bf16[128,1024]{1,0:T(8,128)(2,1)S(1)} collective-permute-done((bf16[128,1024]{1,0:T(8,128)(2,1)S(1)}, bf16[128,1024]{1,0:T(8,128)(2,1)S(1)}, u32[]{:S(2)}, u32[]{:S(2)}) %collective-permute-start.7) | collective-permute-done | bytes 262176 | tf_op jit(solution)/shard_map/ppermute | solution.py:14
  94.8 12.5 %collective-permute-done.8 = bf16[128,1024]{1,0:T(8,128)(2,1)S(1)} collective-permute-done((bf16[128,1024]{1,0:T(8,128)(2,1)S(1)}, bf16[128,1024]{1,0:T(8,128)(2,1)S(1)}, u32[]{:S(2)}, u32[]{:S(2)}) %collective-permute-start.8) | collective-permute-done | bytes 262176 | tf_op jit(solution)/shard_map/ppermute | solution.py:14
  108.0 11.9 %collective-permute-done.9 = bf16[128,1024]{1,0:T(8,128)(2,1)S(1)} collective-permute-done((bf16[128,1024]{1,0:T(8,128)(2,1)S(1)}, bf16[128,1024]{1,0:T(8,128)(2,1)S(1)}, u32[]{:S(2)}, u32[]{:S(2)}) %collective-permute-start.9) | collective-permute-done | bytes 262176 | tf_op jit(solution)/shard_map/ppermute | solution.py:14
  120.7 11.1 %collective-permute-done.10 = bf16[128,1024]{1,0:T(8,128)(2,1)S(1)} collective-permute-done((bf16[128,1024]{1,0:T(8,128)(2,1)S(1)}, bf16[128,1024]{1,0:T(8,128)(2,1)S(1)}, u32[]{:S(2)}, u32[]{:S(2)}) %collective-permute-start.10) | collective-permute-done | bytes 262176 | tf_op jit(solution)/shard_map/ppermute | solution.py:14
  132.5 10.2 %collective-permute-done.11 = bf16[128,1024]{1,0:T(8,128)(2,1)S(1)} collective-permute-done((bf16[128,1024]{1,0:T(8,128)(2,1)S(1)}, bf16[128,1024]{1,0:T(8,128)(2,1)S(1)}, u32[]{:S(2)}, u32[]{:S(2)}) %collective-permute-start.11) | collective-permute-done | bytes 262176 | tf_op jit(solution)/shard_map/ppermute | solution.py:14
  143.3 10.0 %collective-permute-done.12 = bf16[128,1024]{1,0:T(8,128)(2,1)S(1)} collective-permute-done((bf16[128,1024]{1,0:T(8,128)(2,1)S(1)}, bf16[128,1024]{1,0:T(8,128)(2,1)S(1)}, u32[]{:S(2)}, u32[]{:S(2)}) %collective-permute-start.12) | collective-permute-done | bytes 262176 | tf_op jit(solution)/shard_map/ppermute | solution.py:14
  154.0 10.1 %collective-permute-done.13 = bf16[128,1024]{1,0:T(8,128)(2,1)} collective-permute-done((bf16[128,1024]{1,0:T(8,128)(2,1)S(1)}, bf16[128,1024]{1,0:T(8,128)(2,1)}, u32[]{:S(2)}, u32[]{:S(2)}) %collective-permute-start.13) | collective-permute-done | bytes 262176 | tf_op jit(solution)/shard_map/ppermute | solution.py:14
  166.3 8.1 %collective-permute-done.14 = bf16[128,1024]{1,0:T(8,128)(2,1)} collective-permute-done((bf16[128,1024]{1,0:T(8,128)(2,1)}, bf16[128,1024]{1,0:T(8,128)(2,1)}, u32[]{:S(2)}, u32[]{:S(2)}) %collective-permute-start.14) | collective-permute-done | bytes 262176 | tf_op jit(solution)/shard_map/ppermute | solution.py:14
  184.8 3.2 copy-done.13
  189.3 2.8 fusion.20
  193.8 4.5 %compare_select_fusion.4 = (s32[256,1]{0,1:T(1,128)S(1)}, s32[256,1]{0,1:T(1,128)S(1)}) fusion(s32[]{:T(128)} %bitcast.13, s32[]{:T(128)} %bitcast.14, s32[]{:T(128)} %bitcast.15, s32[]{:T(128)} %bitcast.16, s32[]{:T(128)} %bitcast.17, s32[]{:T(128)} %bitcast.19, s32[]{:T(128)} %bitcast.18, s32[1,256,1]{1,2,0:T(1,128)S(1)} %copy-done.12), kind=kLoop, calls=%fused_computation.76 | loop fusion | flops 3840 | bytes 3100 | tf_op jit(solution)/shard_map/gather | solution.py:63
  198.9 36.1 %scatter_fusion = s32[16,48]{1,0:T(8,128)} fusion(s32[16,48]{1,0:T(8,128)} %broadcast.106, s32[256]{0:T(256)S(1)} %bitcast.67, s32[256]{0:T(256)S(1)} %bitcast.75), kind=kCustom, calls=%fused_computation.2 | custom fusion | bytes 5120 | tf_op jit(solution)/shard_map/scatter | solution.py:53
  235.1 3.5 all-to-all-start
  239.9 36.8 %scatter_fusion.1 = bf16[16,48,1024]{2,1,0:T(8,128)(2,1)} fusion(bf16[16,48,1024]{2,1,0:T(8,128)(2,1)} %broadcast_in_dim.22, s32[256]{0:T(256)S(1)} %bitcast.68, bf16[256,1024]{1,0:T(8,128)(2,1)S(1)} %get-tuple-element.32), kind=kCustom, calls=%fused_computation.3 | custom fusion | bytes 1574912 | tf_op jit(solution)/shard_map/scatter | solution.py:50
  276.8 6.9 %all-to-all-start.1 = ((bf16[16,48,1024]{2,1,0:T(8,128)(2,1)}), bf16[16,48,1024]{2,1,0:T(8,128)(2,1)S(1)}, u32[]{:S(2)}, u32[]{:S(2)}) async-start(bf16[16,48,1024]{2,1,0:T(8,128)(2,1)} %scatter_fusion.1), calls=%async_computation.2 | async-start | bytes 3145728 | tf_op jit(solution)/shard_map/all_to_all | solution.py:56
  283.8 4.6 %fusion.12 = bf16[256,1024]{0,1:T(8,128)(2,1)} fusion(bf16[4096,1024]{1,0:T(8,128)(2,1)} %copy-done.13, s32[]{:T(128)S(6)} %select_n.82, bf16[1,256,2048]{2,1,0:T(8,128)(2,1)} %param.7), kind=kOutput, calls=%fused_computation.13 | convolution fusion | flops 1074003968 | bytes 5767172 | tf_op jit(solution)/shard_map/dot_general | solution.py:34
  289.7 3.6 gather_fusion
  293.3 14.9 %all-to-all-done.1 = bf16[16,48,1024]{2,1,0:T(8,128)(2,1)S(1)} async-done(((bf16[16,48,1024]{2,1,0:T(8,128)(2,1)}), bf16[16,48,1024]{2,1,0:T(8,128)(2,1)S(1)}, u32[]{:S(2)}, u32[]{:S(2)}) %all-to-all-start.1) | async-done | bytes 1572896 | tf_op jit(solution)/shard_map/all_to_all | solution.py:56
  308.3 2.0 fusion.5
  311.6 6.3 %all-to-all-start.2 = ((f32[16,1,48]{2,1,0:T(1,128)}), f32[16,1,48]{2,1,0:T(1,128)S(1)}, u32[]{:S(2)}, u32[]{:S(2)}) async-start(f32[16,1,48]{2,1,0:T(1,128)} %compare_select_fusion), calls=%async_computation.3 | async-start | bytes 16384 | tf_op jit(solution)/shard_map/all_to_all | solution.py:62
  318.6 5.7 %select_select_fusion = s32[256]{0:T(256)S(1)} fusion(pred[256]{0:T(512)(128)(4,1)S(1)} %get-tuple-element.10, pred[256]{0:T(512)(128)(4,1)S(1)} %get-tuple-element.9, pred[256]{0:T(512)(128)(4,1)S(1)} %get-tuple-element.8, pred[256]{0:T(512)(128)(4,1)S(1)} %get-tuple-element.7, pred[256]{0:T(512)(128)(4,1)S(1)} %get-tuple-element.6, ...), kind=kLoop, calls=%fused_computation.87 | loop fusion | flops 2304 | bytes 4388 | tf_op jit(solution)/shard_map/gather | solution.py:63
  325.6 40.7 %psum.15 = f32[1024]{0:T(1024)S(1)} all-reduce(f32[1024]{0:T(1024)S(1)} %get-tuple-element.31), channel_id=1, replica_groups=mesh['inner'=16,'outer'=2] {'inner','outer'}, use_global_device_ids=true, to_apply=%region_3.4 | all-reduce | flops 1024 | bytes 8192 | tf_op jit(solution)/shard_map/psum | solution.py:67
  366.4 1.9 gather_fusion.1
  369.6 1.8 subtract_divide_fusion
  (109 shorter events, 26.2 us)
Async XLA Ops:
  7.2 180.8 %copy-start = (bf16[1,256,2048]{2,1,0:T(8,128)(2,1)S(1)}, bf16[1,256,2048]{2,1,0:T(8,128)(2,1)}, u32[]{:S(2)}) copy-start(bf16[1,256,2048]{2,1,0:T(8,128)(2,1)} %param.6) | copy-start | bytes 3145732
  7.2 177.5 %copy-start.1 = (bf16[128,1024]{1,0:T(8,128)(2,1)S(1)}, bf16[128,1024]{1,0:T(8,128)(2,1)}, u32[]{:S(2)}) copy-start(bf16[128,1024]{1,0:T(8,128)(2,1)} %param.8) | copy-start | bytes 786436
  7.2 310.8 %reduce-scatter.2.cloned.1.call-start = ((), (), s32[]{:S(2)}) async-start(), calls=%async_computation.4 | async-start | bytes 4456448 | tf_op jit(solution)/shard_map/reduce_scatter | solution.py:70
  7.2 13.5 %collective-permute-start = (bf16[128,1024]{1,0:T(8,128)(2,1)}, bf16[128,1024]{1,0:T(8,128)(2,1)S(1)}, u32[]{:S(2)}, u32[]{:S(2)}) collective-permute-start(bf16[128,1024]{1,0:T(8,128)(2,1)} %param.8), channel_id=1, source_target_pairs={{0,2},{2,4},{4,6},{6,8},{8,10},{10,12},{12,14},{14,16},{16,18},{18... | collective-permute-start | bytes 786440 | tf_op jit(solution)/shard_map/ppermute | solution.py:14
  20.7 11.1 %collective-permute-start.1 = (bf16[128,1024]{1,0:T(8,128)(2,1)S(1)}, bf16[128,1024]{1,0:T(8,128)(2,1)S(1)}, u32[]{:S(2)}, u32[]{:S(2)}) collective-permute-start(bf16[128,1024]{1,0:T(8,128)(2,1)S(1)} %collective-permute-done), channel_id=1, source_target_pairs={{0,2},{2,4},{4,6},{6,8},{8,10},{10,12},{12,14},{14,16},{16,18},{18... | collective-permute-start | bytes 786440 | tf_op jit(solution)/shard_map/ppermute | solution.py:14
  31.8 10.2 %collective-permute-start.2 = (bf16[128,1024]{1,0:T(8,128)(2,1)S(1)}, bf16[128,1024]{1,0:T(8,128)(2,1)S(1)}, u32[]{:S(2)}, u32[]{:S(2)}) collective-permute-start(bf16[128,1024]{1,0:T(8,128)(2,1)S(1)} %collective-permute-done.1), channel_id=1, source_target_pairs={{0,2},{2,4},{4,6},{6,8},{8,10},{10,12},{12,14},{14,16},{16,18},{18... | collective-permute-start | bytes 786440 | tf_op jit(solution)/shard_map/ppermute | solution.py:14
  42.0 10.0 %collective-permute-start.3 = (bf16[128,1024]{1,0:T(8,128)(2,1)S(1)}, bf16[128,1024]{1,0:T(8,128)(2,1)S(1)}, u32[]{:S(2)}, u32[]{:S(2)}) collective-permute-start(bf16[128,1024]{1,0:T(8,128)(2,1)S(1)} %collective-permute-done.2), channel_id=1, source_target_pairs={{0,2},{2,4},{4,6},{6,8},{8,10},{10,12},{12,14},{14,16},{16,18},{18... | collective-permute-start | bytes 786440 | tf_op jit(solution)/shard_map/ppermute | solution.py:14
  52.0 10.0 %collective-permute-start.4 = (bf16[128,1024]{1,0:T(8,128)(2,1)S(1)}, bf16[128,1024]{1,0:T(8,128)(2,1)S(1)}, u32[]{:S(2)}, u32[]{:S(2)}) collective-permute-start(bf16[128,1024]{1,0:T(8,128)(2,1)S(1)} %collective-permute-done.3), channel_id=1, source_target_pairs={{0,2},{2,4},{4,6},{6,8},{8,10},{10,12},{12,14},{14,16},{16,18},{18... | collective-permute-start | bytes 786440 | tf_op jit(solution)/shard_map/ppermute | solution.py:14
  61.9 10.0 %collective-permute-start.5 = (bf16[128,1024]{1,0:T(8,128)(2,1)S(1)}, bf16[128,1024]{1,0:T(8,128)(2,1)S(1)}, u32[]{:S(2)}, u32[]{:S(2)}) collective-permute-start(bf16[128,1024]{1,0:T(8,128)(2,1)S(1)} %collective-permute-done.4), channel_id=1, source_target_pairs={{0,2},{2,4},{4,6},{6,8},{8,10},{10,12},{12,14},{14,16},{16,18},{18... | collective-permute-start | bytes 786440 | tf_op jit(solution)/shard_map/ppermute | solution.py:14
  71.9 10.9 %collective-permute-start.6 = (bf16[128,1024]{1,0:T(8,128)(2,1)S(1)}, bf16[128,1024]{1,0:T(8,128)(2,1)S(1)}, u32[]{:S(2)}, u32[]{:S(2)}) collective-permute-start(bf16[128,1024]{1,0:T(8,128)(2,1)S(1)} %collective-permute-done.5), channel_id=1, source_target_pairs={{0,2},{2,4},{4,6},{6,8},{8,10},{10,12},{12,14},{14,16},{16,18},{18... | collective-permute-start | bytes 786440 | tf_op jit(solution)/shard_map/ppermute | solution.py:14
  82.8 12.1 %collective-permute-start.7 = (bf16[128,1024]{1,0:T(8,128)(2,1)S(1)}, bf16[128,1024]{1,0:T(8,128)(2,1)S(1)}, u32[]{:S(2)}, u32[]{:S(2)}) collective-permute-start(bf16[128,1024]{1,0:T(8,128)(2,1)S(1)} %collective-permute-done.6), channel_id=1, source_target_pairs={{0,2},{2,4},{4,6},{6,8},{8,10},{10,12},{12,14},{14,16},{16,18},{18... | collective-permute-start | bytes 786440 | tf_op jit(solution)/shard_map/ppermute | solution.py:14
  94.8 12.5 %collective-permute-start.8 = (bf16[128,1024]{1,0:T(8,128)(2,1)S(1)}, bf16[128,1024]{1,0:T(8,128)(2,1)S(1)}, u32[]{:S(2)}, u32[]{:S(2)}) collective-permute-start(bf16[128,1024]{1,0:T(8,128)(2,1)S(1)} %collective-permute-done.7), channel_id=1, source_target_pairs={{0,2},{2,4},{4,6},{6,8},{8,10},{10,12},{12,14},{14,16},{16,18},{18... | collective-permute-start | bytes 786440 | tf_op jit(solution)/shard_map/ppermute | solution.py:14
  108.0 11.9 %collective-permute-start.9 = (bf16[128,1024]{1,0:T(8,128)(2,1)S(1)}, bf16[128,1024]{1,0:T(8,128)(2,1)S(1)}, u32[]{:S(2)}, u32[]{:S(2)}) collective-permute-start(bf16[128,1024]{1,0:T(8,128)(2,1)S(1)} %collective-permute-done.8), channel_id=1, source_target_pairs={{0,2},{2,4},{4,6},{6,8},{8,10},{10,12},{12,14},{14,16},{16,18},{18... | collective-permute-start | bytes 786440 | tf_op jit(solution)/shard_map/ppermute | solution.py:14
  120.7 11.1 %collective-permute-start.10 = (bf16[128,1024]{1,0:T(8,128)(2,1)S(1)}, bf16[128,1024]{1,0:T(8,128)(2,1)S(1)}, u32[]{:S(2)}, u32[]{:S(2)}) collective-permute-start(bf16[128,1024]{1,0:T(8,128)(2,1)S(1)} %collective-permute-done.9), channel_id=1, source_target_pairs={{0,2},{2,4},{4,6},{6,8},{8,10},{10,12},{12,14},{14,16},{16,18},{18... | collective-permute-start | bytes 786440 | tf_op jit(solution)/shard_map/ppermute | solution.py:14
  132.5 10.2 %collective-permute-start.11 = (bf16[128,1024]{1,0:T(8,128)(2,1)S(1)}, bf16[128,1024]{1,0:T(8,128)(2,1)S(1)}, u32[]{:S(2)}, u32[]{:S(2)}) collective-permute-start(bf16[128,1024]{1,0:T(8,128)(2,1)S(1)} %collective-permute-done.10), channel_id=1, source_target_pairs={{0,2},{2,4},{4,6},{6,8},{8,10},{10,12},{12,14},{14,16},{16,18},{18... | collective-permute-start | bytes 786440 | tf_op jit(solution)/shard_map/ppermute | solution.py:14
  142.6 0.7 copy-start.8
  143.3 10.0 %collective-permute-start.12 = (bf16[128,1024]{1,0:T(8,128)(2,1)S(1)}, bf16[128,1024]{1,0:T(8,128)(2,1)S(1)}, u32[]{:S(2)}, u32[]{:S(2)}) collective-permute-start(bf16[128,1024]{1,0:T(8,128)(2,1)S(1)} %collective-permute-done.11), channel_id=1, source_target_pairs={{0,2},{2,4},{4,6},{6,8},{8,10},{10,12},{12,14},{14,16},{16,18},{18... | collective-permute-start | bytes 786440 | tf_op jit(solution)/shard_map/ppermute | solution.py:14
  154.0 10.1 %collective-permute-start.13 = (bf16[128,1024]{1,0:T(8,128)(2,1)S(1)}, bf16[128,1024]{1,0:T(8,128)(2,1)}, u32[]{:S(2)}, u32[]{:S(2)}) collective-permute-start(bf16[128,1024]{1,0:T(8,128)(2,1)S(1)} %collective-permute-done.12), channel_id=1, source_target_pairs={{0,2},{2,4},{4,6},{6,8},{8,10},{10,12},{12,14},{14,16},{16,18},{18... | collective-permute-start | bytes 786440 | tf_op jit(solution)/shard_map/ppermute | solution.py:14
  164.1 10.3 %collective-permute-start.14 = (bf16[128,1024]{1,0:T(8,128)(2,1)}, bf16[128,1024]{1,0:T(8,128)(2,1)}, u32[]{:S(2)}, u32[]{:S(2)}) collective-permute-start(bf16[128,1024]{1,0:T(8,128)(2,1)} %collective-permute-done.13), channel_id=1, source_target_pairs={{0,2},{2,4},{4,6},{6,8},{8,10},{10,12},{12,14},{14,16},{16,18},{18... | collective-permute-start | bytes 786440 | tf_op jit(solution)/shard_map/ppermute | solution.py:14
  164.1 20.2 %copy-start.11 = (bf16[128,1024]{1,0:T(8,128)(2,1)S(1)}, bf16[128,1024]{1,0:T(8,128)(2,1)}, u32[]{:S(2)}) copy-start(bf16[128,1024]{1,0:T(8,128)(2,1)} %copy-done.10) | copy-start | bytes 786436
  164.1 20.3 %copy-start.9 = (bf16[128,1024]{1,0:T(8,128)(2,1)S(1)}, bf16[128,1024]{1,0:T(8,128)(2,1)}, u32[]{:S(2)}) copy-start(bf16[128,1024]{1,0:T(8,128)(2,1)} %copy-done.8) | copy-start | bytes 786436
  164.1 20.3 %copy-start.7 = (bf16[128,1024]{1,0:T(8,128)(2,1)S(1)}, bf16[128,1024]{1,0:T(8,128)(2,1)}, u32[]{:S(2)}) copy-start(bf16[128,1024]{1,0:T(8,128)(2,1)} %copy-done.6) | copy-start | bytes 786436
  164.1 20.3 %copy-start.5 = (bf16[128,1024]{1,0:T(8,128)(2,1)S(1)}, bf16[128,1024]{1,0:T(8,128)(2,1)}, u32[]{:S(2)}) copy-start(bf16[128,1024]{1,0:T(8,128)(2,1)} %copy-done.4) | copy-start | bytes 786436
  164.1 20.4 %copy-start.3 = (bf16[128,1024]{1,0:T(8,128)(2,1)S(1)}, bf16[128,1024]{1,0:T(8,128)(2,1)}, u32[]{:S(2)}) copy-start(bf16[128,1024]{1,0:T(8,128)(2,1)} %copy-done.2) | copy-start | bytes 786436
  184.7 7.4 %copy-start.12 = (s32[1,256,1]{1,2,0:T(1,128)S(1)}, s32[1,256,1]{1,2,0:T(1,128)}, u32[]{:S(2)}) copy-start(s32[1,256,1]{1,2,0:T(1,128)} %param.10) | copy-start | bytes 3076
  184.7 8.3 %copy-start.15 = (s32[2,16]{1,0:T(2,128)S(1)}, s32[2,16]{1,0:T(2,128)}, u32[]{:S(2)}) copy-start(s32[2,16]{1,0:T(2,128)} %param.9) | copy-start | bytes 388
  184.8 3.2 copy-start.13
  188.0 10.9 %copy-start.14 = (s32[1,256]{1,0:T(1,128)S(1)}, s32[1,256]{1,0:T(1,128)}, u32[]{:S(2)}) copy-start(s32[1,256]{1,0:T(1,128)} %param.11) | copy-start | bytes 3076
  235.1 41.7 %all-to-all-start = ((s32[16,1,48]{2,1,0:T(1,128)}), s32[16,1,48]{2,1,0:T(1,128)S(1)}, u32[]{:S(2)}, u32[]{:S(2)}) async-start(s32[16,1,48]{2,1,0:T(1,128)} %bitcast.29), calls=%async_computation.1 | async-start | bytes 16384 | tf_op jit(solution)/shard_map/all_to_all | solution.py:57
  276.8 31.5 %all-to-all-start.1 = ((bf16[16,48,1024]{2,1,0:T(8,128)(2,1)}), bf16[16,48,1024]{2,1,0:T(8,128)(2,1)S(1)}, u32[]{:S(2)}, u32[]{:S(2)}) async-start(bf16[16,48,1024]{2,1,0:T(8,128)(2,1)} %scatter_fusion.1), calls=%async_computation.2 | async-start | bytes 3145728 | tf_op jit(solution)/shard_map/all_to_all | solution.py:56
  311.6 54.8 %all-to-all-start.2 = ((f32[16,1,48]{2,1,0:T(1,128)}), f32[16,1,48]{2,1,0:T(1,128)S(1)}, u32[]{:S(2)}, u32[]{:S(2)}) async-start(f32[16,1,48]{2,1,0:T(1,128)} %compare_select_fusion), calls=%async_computation.3 | async-start | bytes 16384 | tf_op jit(solution)/shard_map/all_to_all | solution.py:62
  317.9 51.7 %all-reduce.2.cloned.1.call-start = ((), (), s32[]{:S(2)}) async-start(), calls=%async_computation.5 | async-start | bytes 524288 | tf_op jit(solution)/shard_map/psum | solution.py:78
  (4 other events, 2.8 us)
Sparse Core Ops, SparseCore 0:
  192.3 99.0 reduce-scatter.1
  321.1 19.5 all-reduce.1
